TPU v7x, 512 devices: a whole 4x4x16 slice. The times are simulated.
512 devices in a mesh: cuts: 32 (over z, x_lo), blk: 16 (over x_hi, y, core).
Axes of the slice: x: 4 (x_hi: 2, x_lo: 2; x = x_hi * 2 + x_lo), y: 4, z: 16, core: 2. Of those that a mesh axis runs over, the one named last changes fastest.
Arguments:
- steps: bfloat16 [512, 2, 512, 512], P(('cuts', 'blk')), as said below
Outputs:
- sidebands: float32 [32, 2, 512, 512], P(None, None, 'blk', 'cuts')
Inputs may be any that keep to these rules, and one draw needn't show every extreme that they name: `steps`: sqrt(512) times every entry lies between -1 and 1.
All inputs are finite; a program needn't handle non-finite values.
Results may differ from a plain program's by a relative error of at most 0.035.
Values may be sent and summed in bfloat16 or wider, within the bound.
A program may use at most 64 MiB of HBM per device.

v0:
```python
import math
import jax
import jax.numpy as jnp
from jax import lax
from jax.sharding import PartitionSpec as P


def from_partner(block, axis, distance):
    count = lax.axis_size(axis)
    route = []
    for low in range(count):
        high = low | 1 << distance
        if high != low and high < count:
            route += [(low, high), (high, low)]
    return lax.ppermute(block, axis, route)


def passed_along(x, axis, by):
    devices = lax.axis_size(axis)
    return lax.ppermute(x, axis, [(i, (i + by) % devices) for i in range(devices)])


def complex_product(left_factor, right_factor):
    real_real = jnp.dot(left_factor[0], right_factor[0], preferred_element_type=jnp.float32)
    imag_imag = jnp.dot(left_factor[1], right_factor[1], preferred_element_type=jnp.float32)
    real_imag = jnp.dot(left_factor[0], right_factor[1], preferred_element_type=jnp.float32)
    imag_real = jnp.dot(left_factor[1], right_factor[0], preferred_element_type=jnp.float32)
    return jnp.stack([real_real - imag_imag, real_imag + imag_real])


def complex_wide(left_factor, right_factor):
    hp = lax.Precision.HIGHEST
    real_real = jnp.dot(left_factor[0], right_factor[0], precision=hp)
    imag_imag = jnp.dot(left_factor[1], right_factor[1], precision=hp)
    real_imag = jnp.dot(left_factor[0], right_factor[1], precision=hp)
    imag_real = jnp.dot(left_factor[1], right_factor[0], precision=hp)
    return jnp.stack([real_real - imag_imag, real_imag + imag_real])


def group_product(left_factor, right_factor):
    if left_factor.dtype == jnp.bfloat16:
        return complex_product(left_factor, right_factor)
    return complex_wide(left_factor, right_factor)


def per_device(steps):
    current = steps[0]
    order = current.shape[-1]
    blk_count = lax.axis_size("blk")
    block_rows = order // blk_count
    tree_depth = blk_count.bit_length() - 1
    blk_index = lax.axis_index("blk")
    first_partner = from_partner(current, "blk", 0)
    for section in range(tree_depth):
        if section == 0:
            partner = first_partner
        else:
            partner = from_partner(current, "blk", section)
        is_upper = blk_index >> section & 1 == 1
        upper_factor = jnp.where(is_upper, current, partner)
        lower_factor = jnp.where(is_upper, partner, current)
        current = group_product(upper_factor, lower_factor)
    current = current.astype(jnp.bfloat16)
    row_block = lax.dynamic_slice_in_dim(current, blk_index * block_rows, block_rows, 1)
    cuts_count = lax.axis_size("cuts")
    loop_depth = cuts_count.bit_length() - 1
    for section in range(loop_depth):
        distance = 1 << section
        ahead = passed_along(row_block, "cuts", -distance)

        def add_rows(running, incoming, offset, ahead=ahead):
            return complex_product(ahead, incoming)

        empty_sum = jnp.zeros(row_block.shape, jnp.float32)
        running = add_rows(
            empty_sum, lax.all_gather(row_block, "blk", axis=1, tiled=True), jnp.int32(0)
        )
        row_block = running.astype(jnp.bfloat16)
    received = lax.all_to_all(row_block[None], "cuts", split_axis=3, concat_axis=0, tiled=True)
    slice_count = received.shape[0]
    freq_index = jnp.arange(slice_count, dtype=jnp.int32)
    phase_angle = (
        2.0
        * math.pi
        / slice_count
        * (freq_index[:, None] * freq_index[None, :] % slice_count).astype(jnp.float32)
    )
    cosine_table = jnp.cos(phase_angle)
    sine_table = jnp.sin(phase_angle)
    flattened = received.astype(jnp.float32).reshape(slice_count, 2, -1)
    hp = lax.Precision.HIGHEST
    real_part = jnp.dot(cosine_table, flattened[:, 0], precision=hp) + jnp.dot(
        sine_table, flattened[:, 1], precision=hp
    )
    imag_part = jnp.dot(cosine_table, flattened[:, 1], precision=hp) - jnp.dot(
        sine_table, flattened[:, 0], precision=hp
    )
    norm_factor = math.sqrt(order / slice_count)
    result = jnp.stack([real_part, imag_part], axis=1) * norm_factor
    return result.reshape(received.shape)


def solution(mesh):
    in_specs = (P(("cuts", "blk"), None, None, None),)
    out_specs = P(None, None, "blk", "cuts")
    return jax.shard_map(
        per_device, mesh=mesh, in_specs=in_specs, out_specs=out_specs, check_vma=False
    )
```

profile of v0, /device:TPU:2, one launch (start us, length us, event | category | flops | bytes accessed | tf_op | source)
XLA Modules:
  0.0 564.4 jit_solution(16650119582925848394)
XLA Ops:
  6.5 1.9 collective-permute-start
  8.5 2.8 collective-permute-done
  11.3 1.4 broadcast_select_fusion.1
  14.4 1.5 pad_maximum_fusion
  15.9 3.5 collective-permute-start.1
  19.4 46.4 %collective-permute-done.1 = f32[2,512,512]{2,1,0:T(8,128)} collective-permute-done((f32[2,512,512]{2,1,0:T(8,128)}, f32[2,512,512]{2,1,0:T(8,128)}, u32[]{:S(2)}, u32[]{:S(2)}) %collective-permute-start.1) | collective-permute-done | bytes 2097184 | tf_op jit(solution)/shard_map/ppermute | solution.py:15
  65.8 2.3 broadcast_select_fusion.3
  68.1 1.8 fusion.31
  70.0 1.8 fusion.30
  71.8 1.8 fusion.3
  73.7 1.8 fusion.2
  75.6 1.5 pad_maximum_fusion.1
  77.1 5.3 collective-permute-start.2
  82.3 45.3 %collective-permute-done.2 = f32[2,512,512]{2,1,0:T(8,128)} collective-permute-done((f32[2,512,512]{2,1,0:T(8,128)}, f32[2,512,512]{2,1,0:T(8,128)}, u32[]{:S(2)}, u32[]{:S(2)}) %collective-permute-start.2) | collective-permute-done | bytes 2097184 | tf_op jit(solution)/shard_map/ppermute | solution.py:15
  127.6 2.3 broadcast_select_fusion.5
  129.9 1.8 fusion.33
  131.8 1.8 fusion.32
  133.7 1.8 fusion.1
  135.5 1.8 fusion
  137.4 1.5 pad_maximum_fusion.2
  138.9 4.2 collective-permute-start.3
  143.1 45.4 %collective-permute-done.3 = f32[2,512,512]{2,1,0:T(8,128)} collective-permute-done((f32[2,512,512]{2,1,0:T(8,128)}, f32[2,512,512]{2,1,0:T(8,128)}, u32[]{:S(2)}, u32[]{:S(2)}) %collective-permute-start.3) | collective-permute-done | bytes 2097184 | tf_op jit(solution)/shard_map/ppermute | solution.py:15
  188.5 2.3 broadcast_select_fusion.6
  190.8 1.9 fusion.34
  192.7 1.9 fusion.35
  194.6 1.9 fusion.8
  196.4 1.9 fusion.9
  199.1 7.8 %collective-permute-start.4 = (bf16[2,32,512]{2,1,0:T(8,128)(2,1)}, bf16[2,32,512]{2,1,0:T(8,128)(2,1)S(1)}, u32[]{:S(2)}, u32[]{:S(2)}) collective-permute-start(bf16[2,32,512]{2,1,0:T(8,128)(2,1)} %fusion.50), channel_id=1, source_target_pairs={{0,496},{16,0},{32,16},{48,32},{64,48},{80,64},{96,80},{112,96},{1... | collective-permute-start | bytes 196616 | tf_op jit(solution)/shard_map/ppermute | solution.py:20
  206.9 2.2 collective-permute-done.4
  209.1 53.8 %all-gather.6.cloned.1.call-done = bf16[2,512,512]{2,1,0:T(8,128)(2,1)} async-done(((bf16[2,32,512]{2,1,0:T(8,128)(2,1)}), bf16[2,512,512]{2,1,0:T(8,128)(2,1)}) %all-gather.6.cloned.1.call-update) | async-done | bytes 1048592 | tf_op jit(solution)/shard_map/all_gather | solution.py:76
  262.9 1.2 fusion.39
  264.1 1.2 fusion.38
  265.4 1.2 fusion.29
  266.6 1.2 fusion.28
  268.6 6.0 %collective-permute-start.5 = (bf16[2,32,512]{2,1,0:T(8,128)(2,1)}, bf16[2,32,512]{2,1,0:T(8,128)(2,1)S(1)}, u32[]{:S(2)}, u32[]{:S(2)}) collective-permute-start(bf16[2,32,512]{2,1,0:T(8,128)(2,1)} %pad_maximum_fusion.3), channel_id=1, source_target_pairs={{0,480},{16,496},{32,0},{48,16},{64,32},{80,48},{96,64},{112,80},{... | collective-permute-start | bytes 196616 | tf_op jit(solution)/shard_map/ppermute | solution.py:20
  274.5 2.2 collective-permute-done.5
  276.7 51.0 %all-gather.8.cloned.1.call-done = bf16[2,512,512]{2,1,0:T(8,128)(2,1)} async-done(((bf16[2,32,512]{2,1,0:T(8,128)(2,1)}), bf16[2,512,512]{2,1,0:T(8,128)(2,1)}) %all-gather.8.cloned.1.call-update) | async-done | bytes 1048592 | tf_op jit(solution)/shard_map/all_gather | solution.py:76
  327.7 1.2 fusion.41
  328.9 1.2 fusion.40
  330.1 1.2 fusion.27
  331.4 1.2 fusion.26
  333.3 6.8 %collective-permute-start.6 = (bf16[2,32,512]{2,1,0:T(8,128)(2,1)}, bf16[2,32,512]{2,1,0:T(8,128)(2,1)S(1)}, u32[]{:S(2)}, u32[]{:S(2)}) collective-permute-start(bf16[2,32,512]{2,1,0:T(8,128)(2,1)} %pad_maximum_fusion.4), channel_id=1, source_target_pairs={{0,448},{16,464},{32,480},{48,496},{64,0},{80,16},{96,32},{112,48}... | collective-permute-start | bytes 196616 | tf_op jit(solution)/shard_map/ppermute | solution.py:20
  340.1 3.5 collective-permute-done.6
  343.6 48.8 %all-gather.10.cloned.1.call-done = bf16[2,512,512]{2,1,0:T(8,128)(2,1)} async-done(((bf16[2,32,512]{2,1,0:T(8,128)(2,1)}), bf16[2,512,512]{2,1,0:T(8,128)(2,1)}) %all-gather.10.cloned.1.call-update) | async-done | bytes 1048592 | tf_op jit(solution)/shard_map/all_gather | solution.py:76
  392.5 1.2 fusion.43
  393.7 1.2 fusion.42
  394.9 1.2 fusion.25
  396.2 1.2 fusion.24
  398.1 8.4 %collective-permute-start.7 = (bf16[2,32,512]{2,1,0:T(8,128)(2,1)}, bf16[2,32,512]{2,1,0:T(8,128)(2,1)S(1)}, u32[]{:S(2)}, u32[]{:S(2)}) collective-permute-start(bf16[2,32,512]{2,1,0:T(8,128)(2,1)} %pad_maximum_fusion.5), channel_id=1, source_target_pairs={{0,384},{16,400},{32,416},{48,432},{64,448},{80,464},{96,480},{112... | collective-permute-start | bytes 196616 | tf_op jit(solution)/shard_map/ppermute | solution.py:20
  406.5 6.3 %collective-permute-done.7 = bf16[2,32,512]{2,1,0:T(8,128)(2,1)S(1)} collective-permute-done((bf16[2,32,512]{2,1,0:T(8,128)(2,1)}, bf16[2,32,512]{2,1,0:T(8,128)(2,1)S(1)}, u32[]{:S(2)}, u32[]{:S(2)}) %collective-permute-start.7) | collective-permute-done | bytes 65568 | tf_op jit(solution)/shard_map/ppermute | solution.py:20
  412.8 44.4 %all-gather.12.cloned.1.call-done = bf16[2,512,512]{2,1,0:T(8,128)(2,1)} async-done(((bf16[2,32,512]{2,1,0:T(8,128)(2,1)}), bf16[2,512,512]{2,1,0:T(8,128)(2,1)}) %all-gather.12.cloned.1.call-update) | async-done | bytes 1048592 | tf_op jit(solution)/shard_map/all_gather | solution.py:76
  457.2 1.2 fusion.45
  458.5 1.2 fusion.44
  459.7 1.2 fusion.23
  460.9 1.2 fusion.22
  462.9 12.8 %collective-permute-start.8 = (bf16[2,32,512]{2,1,0:T(8,128)(2,1)}, bf16[2,32,512]{2,1,0:T(8,128)(2,1)S(1)}, u32[]{:S(2)}, u32[]{:S(2)}) collective-permute-start(bf16[2,32,512]{2,1,0:T(8,128)(2,1)} %pad_maximum_fusion.6), channel_id=1, source_target_pairs={{0,256},{16,272},{32,288},{48,304},{64,320},{80,336},{96,352},{112... | collective-permute-start | bytes 196616 | tf_op jit(solution)/shard_map/ppermute | solution.py:20
  475.7 3.0 collective-permute-done.8
  478.7 43.3 %all-gather.14.cloned.1.call-done = bf16[2,512,512]{2,1,0:T(8,128)(2,1)} async-done(((bf16[2,32,512]{2,1,0:T(8,128)(2,1)}), bf16[2,512,512]{2,1,0:T(8,128)(2,1)}) %all-gather.14.cloned.1.call-update) | async-done | bytes 1048592 | tf_op jit(solution)/shard_map/all_gather | solution.py:76
  522.0 1.2 fusion.47
  523.3 1.2 fusion.46
  524.5 1.2 fusion.21
  525.7 1.2 fusion.20
  527.4 27.2 %all_to_all.15 = bf16[32,2,512]{2,1,0:T(2,128)(2,1)S(1)} all-to-all(bf16[32,2,512]{2,1,0:T(2,128)(2,1)S(1)} %reshape.43), channel_id=1, replica_groups=mesh['cuts'=32,'blk'=16] {'cuts'}, dimensions={0} | all-to-all | bytes 131072 | tf_op jit(solution)/shard_map/all_to_all | solution.py:79
  556.6 1.3 copy.18
  (32 shorter events, 7.6 us)
Async XLA Ops:
  6.5 256.4 %all-gather.6.cloned.1.call-start = ((), (), s32[]{:S(2)}) async-start(), calls=%async_computation.1 | async-start | bytes 1114112 | tf_op jit(solution)/shard_map/all_gather | solution.py:76
  6.5 4.8 collective-permute-start
  15.9 49.9 %collective-permute-start.1 = (f32[2,512,512]{2,1,0:T(8,128)}, f32[2,512,512]{2,1,0:T(8,128)}, u32[]{:S(2)}, u32[]{:S(2)}) collective-permute-start(f32[2,512,512]{2,1,0:T(8,128)} %pad_maximum_fusion), channel_id=1, source_target_pairs={{0,2},{2,0},{1,3},{3,1},{4,6},{6,4},{5,7},{7,5},{8,10},{10,8},{9,1... | collective-permute-start | bytes 6291464 | tf_op jit(solution)/shard_map/ppermute | solution.py:15
  77.1 50.5 %collective-permute-start.2 = (f32[2,512,512]{2,1,0:T(8,128)}, f32[2,512,512]{2,1,0:T(8,128)}, u32[]{:S(2)}, u32[]{:S(2)}) collective-permute-start(f32[2,512,512]{2,1,0:T(8,128)} %pad_maximum_fusion.1), channel_id=1, source_target_pairs={{0,4},{4,0},{1,5},{5,1},{2,6},{6,2},{3,7},{7,3},{8,12},{12,8},{9,1... | collective-permute-start | bytes 6291464 | tf_op jit(solution)/shard_map/ppermute | solution.py:15
  138.9 49.6 %collective-permute-start.3 = (f32[2,512,512]{2,1,0:T(8,128)}, f32[2,512,512]{2,1,0:T(8,128)}, u32[]{:S(2)}, u32[]{:S(2)}) collective-permute-start(f32[2,512,512]{2,1,0:T(8,128)} %pad_maximum_fusion.2), channel_id=1, source_target_pairs={{0,8},{8,0},{1,9},{9,1},{2,10},{10,2},{3,11},{11,3},{4,12},{12,4},... | collective-permute-start | bytes 6291464 | tf_op jit(solution)/shard_map/ppermute | solution.py:15
  199.0 128.7 %all-gather.8.cloned.1.call-start = ((), (), s32[]{:S(2)}) async-start(), calls=%async_computation.2 | async-start | bytes 1114112 | tf_op jit(solution)/shard_map/all_gather | solution.py:76
  199.1 10.0 %collective-permute-start.4 = (bf16[2,32,512]{2,1,0:T(8,128)(2,1)}, bf16[2,32,512]{2,1,0:T(8,128)(2,1)S(1)}, u32[]{:S(2)}, u32[]{:S(2)}) collective-permute-start(bf16[2,32,512]{2,1,0:T(8,128)(2,1)} %fusion.50), channel_id=1, source_target_pairs={{0,496},{16,0},{32,16},{48,32},{64,48},{80,64},{96,80},{112,96},{1... | collective-permute-start | bytes 196616 | tf_op jit(solution)/shard_map/ppermute | solution.py:20
  268.5 123.9 %all-gather.10.cloned.1.call-start = ((), (), s32[]{:S(2)}) async-start(), calls=%async_computation.3 | async-start | bytes 1114112 | tf_op jit(solution)/shard_map/all_gather | solution.py:76
  268.6 8.2 %collective-permute-start.5 = (bf16[2,32,512]{2,1,0:T(8,128)(2,1)}, bf16[2,32,512]{2,1,0:T(8,128)(2,1)S(1)}, u32[]{:S(2)}, u32[]{:S(2)}) collective-permute-start(bf16[2,32,512]{2,1,0:T(8,128)(2,1)} %pad_maximum_fusion.3), channel_id=1, source_target_pairs={{0,480},{16,496},{32,0},{48,16},{64,32},{80,48},{96,64},{112,80},{... | collective-permute-start | bytes 196616 | tf_op jit(solution)/shard_map/ppermute | solution.py:20
  333.3 123.9 %all-gather.12.cloned.1.call-start = ((), (), s32[]{:S(2)}) async-start(), calls=%async_computation.4 | async-start | bytes 1114112 | tf_op jit(solution)/shard_map/all_gather | solution.py:76
  333.3 10.3 %collective-permute-start.6 = (bf16[2,32,512]{2,1,0:T(8,128)(2,1)}, bf16[2,32,512]{2,1,0:T(8,128)(2,1)S(1)}, u32[]{:S(2)}, u32[]{:S(2)}) collective-permute-start(bf16[2,32,512]{2,1,0:T(8,128)(2,1)} %pad_maximum_fusion.4), channel_id=1, source_target_pairs={{0,448},{16,464},{32,480},{48,496},{64,0},{80,16},{96,32},{112,48}... | collective-permute-start | bytes 196616 | tf_op jit(solution)/shard_map/ppermute | solution.py:20
  398.1 123.9 %all-gather.14.cloned.1.call-start = ((), (), s32[]{:S(2)}) async-start(), calls=%async_computation.5 | async-start | bytes 1114112 | tf_op jit(solution)/shard_map/all_gather | solution.py:76
  398.1 14.7 %collective-permute-start.7 = (bf16[2,32,512]{2,1,0:T(8,128)(2,1)}, bf16[2,32,512]{2,1,0:T(8,128)(2,1)S(1)}, u32[]{:S(2)}, u32[]{:S(2)}) collective-permute-start(bf16[2,32,512]{2,1,0:T(8,128)(2,1)} %pad_maximum_fusion.5), channel_id=1, source_target_pairs={{0,384},{16,400},{32,416},{48,432},{64,448},{80,464},{96,480},{112... | collective-permute-start | bytes 196616 | tf_op jit(solution)/shard_map/ppermute | solution.py:20
  462.9 15.8 %collective-permute-start.8 = (bf16[2,32,512]{2,1,0:T(8,128)(2,1)}, bf16[2,32,512]{2,1,0:T(8,128)(2,1)S(1)}, u32[]{:S(2)}, u32[]{:S(2)}) collective-permute-start(bf16[2,32,512]{2,1,0:T(8,128)(2,1)} %pad_maximum_fusion.6), channel_id=1, source_target_pairs={{0,256},{16,272},{32,288},{48,304},{64,320},{80,336},{96,352},{112... | collective-permute-start | bytes 196616 | tf_op jit(solution)/shard_map/ppermute | solution.py:20
Sparse Core Ops, SparseCore 0:
  199.1 63.7 all-gather.5
  268.6 58.9 all-gather.7
  333.4 58.9 all-gather.9
  398.2 58.9 all-gather.11
  463.0 58.9 all-gather.13
where the time goes:
time: 566 us; the launch traced here: 564 us
  waiting for transfers between devices  398 us (70%)
  starting transfers between devices  56.8 us (10%)
  matrix products  49.7 us (9%)
  blocking collectives  27.2 us (5%)
  other arithmetic  16.2 us (3%)
  between operations  13.5 us (2%)
    all_gather x5, waiting for transfers between devices, per_device(): lax.all_gather(row_block, 'blk', axis=1, tiled=True)  241 us
    ppermute x4, waiting for transfers between devices, from_partner(): return lax.ppermute(block, axis, route)  140 us
    ppermute x5, starting transfers between devices, passed_along(): lax.ppermute(x, axis, [(i, (i + by) % devices) for i in range(devices)])  41.7 us
    all_to_all x1, blocking collectives, per_device(): lax.all_to_all(row_block[None], 'cuts', split_axis=3, concat_axis=0, tile...  27.2 us
    ppermute x5, waiting for transfers between devices, passed_along(): lax.ppermute(x, axis, [(i, (i + by) % devices) for i in range(devices)])  17.3 us
    ppermute x4, starting transfers between devices, from_partner(): return lax.ppermute(block, axis, route)  14.9 us
  transfers between devices with their start and end apart: 14, of which 14 were waited for; matrix products, arithmetic and copies ran while one was open for 0% of the time, Pallas kernels for 0%

commit v1 on v0

--- a/solution.py
+++ b/solution.py
@@ -76,7 +76,10 @@
             empty_sum, lax.all_gather(row_block, "blk", axis=1, tiled=True), jnp.int32(0)
         )
         row_block = running.astype(jnp.bfloat16)
-    received = lax.all_to_all(row_block[None], "cuts", split_axis=3, concat_axis=0, tiled=True)
+    block_2 = row_block[None]
+    pieces = jnp.split(block_2, lax.axis_size("cuts"), axis=3)
+    got = lax.all_to_all(jnp.stack(pieces), "cuts", 0, 0)
+    received = jnp.concatenate(got, axis=0)
     slice_count = received.shape[0]
     freq_index = jnp.arange(slice_count, dtype=jnp.int32)
     phase_angle = (

time: 566 us -> 568 us (level)
  no operation moved by 1% of the time
where the time goes in v1:
time: 568 us; the launch traced here: 567 us
  waiting for transfers between devices  398 us (70%)
  starting transfers between devices  56.8 us (10%)
  matrix products  49.7 us (9%)
  blocking collectives  27.2 us (5%)
  other arithmetic  18.6 us (3%)
  between operations  13.5 us (2%)
    all_gather x5, waiting for transfers between devices, per_device(): lax.all_gather(row_block, 'blk', axis=1, tiled=True)  241 us
    ppermute x4, waiting for transfers between devices, from_partner(): return lax.ppermute(block, axis, route)  140 us
    ppermute x5, starting transfers between devices, passed_along(): lax.ppermute(x, axis, [(i, (i + by) % devices) for i in range(devices)])  41.7 us
    all_to_all x1, blocking collectives, per_device(): got = lax.all_to_all(jnp.stack(pieces), 'cuts', 0, 0)  27.2 us
    ppermute x5, waiting for transfers between devices, passed_along(): lax.ppermute(x, axis, [(i, (i + by) % devices) for i in range(devices)])  17.3 us
    ppermute x4, starting transfers between devices, from_partner(): return lax.ppermute(block, axis, route)  14.9 us
  transfers between devices with their start and end apart: 14, of which 14 were waited for; matrix products, arithmetic and copies ran while one was open for 0% of the time, Pallas kernels for 0%

profile of v1, /device:TPU:2, one launch (start us, length us, event | category | flops | bytes accessed | tf_op | source)
XLA Modules:
  0.0 566.9 jit_solution(14910349567148379383)
XLA Ops:
  6.5 1.9 collective-permute-start
  8.5 2.8 collective-permute-done
  11.3 1.4 broadcast_select_fusion.1
  14.4 1.5 pad_maximum_fusion
  15.9 3.5 collective-permute-start.1
  19.4 46.4 %collective-permute-done.1 = f32[2,512,512]{2,1,0:T(8,128)} collective-permute-done((f32[2,512,512]{2,1,0:T(8,128)}, f32[2,512,512]{2,1,0:T(8,128)}, u32[]{:S(2)}, u32[]{:S(2)}) %collective-permute-start.1) | collective-permute-done | bytes 2097184 | tf_op jit(solution)/shard_map/ppermute | solution.py:15
  65.8 2.3 broadcast_select_fusion.3
  68.1 1.8 fusion.31
  70.0 1.8 fusion.30
  71.8 1.8 fusion.3
  73.7 1.8 fusion.2
  75.6 1.5 pad_maximum_fusion.1
  77.1 5.3 collective-permute-start.2
  82.3 45.3 %collective-permute-done.2 = f32[2,512,512]{2,1,0:T(8,128)} collective-permute-done((f32[2,512,512]{2,1,0:T(8,128)}, f32[2,512,512]{2,1,0:T(8,128)}, u32[]{:S(2)}, u32[]{:S(2)}) %collective-permute-start.2) | collective-permute-done | bytes 2097184 | tf_op jit(solution)/shard_map/ppermute | solution.py:15
  127.6 2.3 broadcast_select_fusion.5
  129.9 1.8 fusion.33
  131.8 1.8 fusion.32
  133.7 1.8 fusion.1
  135.5 1.8 fusion
  137.4 1.5 pad_maximum_fusion.2
  138.9 4.2 collective-permute-start.3
  143.1 45.4 %collective-permute-done.3 = f32[2,512,512]{2,1,0:T(8,128)} collective-permute-done((f32[2,512,512]{2,1,0:T(8,128)}, f32[2,512,512]{2,1,0:T(8,128)}, u32[]{:S(2)}, u32[]{:S(2)}) %collective-permute-start.3) | collective-permute-done | bytes 2097184 | tf_op jit(solution)/shard_map/ppermute | solution.py:15
  188.5 2.3 broadcast_select_fusion.6
  190.8 1.9 fusion.34
  192.7 1.9 fusion.35
  194.6 1.9 fusion.8
  196.4 1.9 fusion.9
  199.1 7.8 %collective-permute-start.4 = (bf16[2,32,512]{2,1,0:T(8,128)(2,1)}, bf16[2,32,512]{2,1,0:T(8,128)(2,1)S(1)}, u32[]{:S(2)}, u32[]{:S(2)}) collective-permute-start(bf16[2,32,512]{2,1,0:T(8,128)(2,1)} %fusion.50), channel_id=1, source_target_pairs={{0,496},{16,0},{32,16},{48,32},{64,48},{80,64},{96,80},{112,96},{1... | collective-permute-start | bytes 196616 | tf_op jit(solution)/shard_map/ppermute | solution.py:20
  206.9 2.2 collective-permute-done.4
  209.1 53.8 %all-gather.6.cloned.1.call-done = bf16[2,512,512]{2,1,0:T(8,128)(2,1)} async-done(((bf16[2,32,512]{2,1,0:T(8,128)(2,1)}), bf16[2,512,512]{2,1,0:T(8,128)(2,1)}) %all-gather.6.cloned.1.call-update) | async-done | bytes 1048592 | tf_op jit(solution)/shard_map/all_gather | solution.py:76
  262.9 1.2 fusion.39
  264.1 1.2 fusion.38
  265.4 1.2 fusion.29
  266.6 1.2 fusion.28
  268.6 6.0 %collective-permute-start.5 = (bf16[2,32,512]{2,1,0:T(8,128)(2,1)}, bf16[2,32,512]{2,1,0:T(8,128)(2,1)S(1)}, u32[]{:S(2)}, u32[]{:S(2)}) collective-permute-start(bf16[2,32,512]{2,1,0:T(8,128)(2,1)} %pad_maximum_fusion.3), channel_id=1, source_target_pairs={{0,480},{16,496},{32,0},{48,16},{64,32},{80,48},{96,64},{112,80},{... | collective-permute-start | bytes 196616 | tf_op jit(solution)/shard_map/ppermute | solution.py:20
  274.5 2.2 collective-permute-done.5
  276.7 51.0 %all-gather.8.cloned.1.call-done = bf16[2,512,512]{2,1,0:T(8,128)(2,1)} async-done(((bf16[2,32,512]{2,1,0:T(8,128)(2,1)}), bf16[2,512,512]{2,1,0:T(8,128)(2,1)}) %all-gather.8.cloned.1.call-update) | async-done | bytes 1048592 | tf_op jit(solution)/shard_map/all_gather | solution.py:76
  327.7 1.2 fusion.41
  328.9 1.2 fusion.40
  330.1 1.2 fusion.27
  331.4 1.2 fusion.26
  333.3 6.8 %collective-permute-start.6 = (bf16[2,32,512]{2,1,0:T(8,128)(2,1)}, bf16[2,32,512]{2,1,0:T(8,128)(2,1)S(1)}, u32[]{:S(2)}, u32[]{:S(2)}) collective-permute-start(bf16[2,32,512]{2,1,0:T(8,128)(2,1)} %pad_maximum_fusion.4), channel_id=1, source_target_pairs={{0,448},{16,464},{32,480},{48,496},{64,0},{80,16},{96,32},{112,48}... | collective-permute-start | bytes 196616 | tf_op jit(solution)/shard_map/ppermute | solution.py:20
  340.1 3.5 collective-permute-done.6
  343.6 48.8 %all-gather.10.cloned.1.call-done = bf16[2,512,512]{2,1,0:T(8,128)(2,1)} async-done(((bf16[2,32,512]{2,1,0:T(8,128)(2,1)}), bf16[2,512,512]{2,1,0:T(8,128)(2,1)}) %all-gather.10.cloned.1.call-update) | async-done | bytes 1048592 | tf_op jit(solution)/shard_map/all_gather | solution.py:76
  392.5 1.2 fusion.43
  393.7 1.2 fusion.42
  394.9 1.2 fusion.25
  396.2 1.2 fusion.24
  398.1 8.4 %collective-permute-start.7 = (bf16[2,32,512]{2,1,0:T(8,128)(2,1)}, bf16[2,32,512]{2,1,0:T(8,128)(2,1)S(1)}, u32[]{:S(2)}, u32[]{:S(2)}) collective-permute-start(bf16[2,32,512]{2,1,0:T(8,128)(2,1)} %pad_maximum_fusion.5), channel_id=1, source_target_pairs={{0,384},{16,400},{32,416},{48,432},{64,448},{80,464},{96,480},{112... | collective-permute-start | bytes 196616 | tf_op jit(solution)/shard_map/ppermute | solution.py:20
  406.5 6.3 %collective-permute-done.7 = bf16[2,32,512]{2,1,0:T(8,128)(2,1)S(1)} collective-permute-done((bf16[2,32,512]{2,1,0:T(8,128)(2,1)}, bf16[2,32,512]{2,1,0:T(8,128)(2,1)S(1)}, u32[]{:S(2)}, u32[]{:S(2)}) %collective-permute-start.7) | collective-permute-done | bytes 65568 | tf_op jit(solution)/shard_map/ppermute | solution.py:20
  412.8 44.4 %all-gather.12.cloned.1.call-done = bf16[2,512,512]{2,1,0:T(8,128)(2,1)} async-done(((bf16[2,32,512]{2,1,0:T(8,128)(2,1)}), bf16[2,512,512]{2,1,0:T(8,128)(2,1)}) %all-gather.12.cloned.1.call-update) | async-done | bytes 1048592 | tf_op jit(solution)/shard_map/all_gather | solution.py:76
  457.2 1.2 fusion.45
  458.5 1.2 fusion.44
  459.7 1.2 fusion.23
  460.9 1.2 fusion.22
  462.9 12.8 %collective-permute-start.8 = (bf16[2,32,512]{2,1,0:T(8,128)(2,1)}, bf16[2,32,512]{2,1,0:T(8,128)(2,1)S(1)}, u32[]{:S(2)}, u32[]{:S(2)}) collective-permute-start(bf16[2,32,512]{2,1,0:T(8,128)(2,1)} %pad_maximum_fusion.6), channel_id=1, source_target_pairs={{0,256},{16,272},{32,288},{48,304},{64,320},{80,336},{96,352},{112... | collective-permute-start | bytes 196616 | tf_op jit(solution)/shard_map/ppermute | solution.py:20
  475.7 3.0 collective-permute-done.8
  478.7 43.3 %all-gather.14.cloned.1.call-done = bf16[2,512,512]{2,1,0:T(8,128)(2,1)} async-done(((bf16[2,32,512]{2,1,0:T(8,128)(2,1)}), bf16[2,512,512]{2,1,0:T(8,128)(2,1)}) %all-gather.14.cloned.1.call-update) | async-done | bytes 1048592 | tf_op jit(solution)/shard_map/all_gather | solution.py:76
  522.0 1.2 fusion.46
  523.3 1.2 fusion.47
  524.5 1.2 fusion.20
  525.7 1.2 fusion.21
  529.9 27.2 %all_to_all.5 = bf16[32,2,512]{2,1,0:T(2,128)(2,1)S(1)} all-to-all(bf16[32,2,512]{2,1,0:T(2,128)(2,1)S(1)} %reshape.44), channel_id=1, replica_groups=mesh['cuts'=32,'blk'=16] {'cuts'}, dimensions={0} | all-to-all | bytes 131072 | tf_op jit(solution)/shard_map/all_to_all | solution.py:81
  559.2 1.3 copy.16
  (62 shorter events, 10.1 us)
Async XLA Ops:
  6.5 256.4 %all-gather.6.cloned.1.call-start = ((), (), s32[]{:S(2)}) async-start(), calls=%async_computation.1 | async-start | bytes 1114112 | tf_op jit(solution)/shard_map/all_gather | solution.py:76
  6.5 4.8 collective-permute-start
  15.9 49.9 %collective-permute-start.1 = (f32[2,512,512]{2,1,0:T(8,128)}, f32[2,512,512]{2,1,0:T(8,128)}, u32[]{:S(2)}, u32[]{:S(2)}) collective-permute-start(f32[2,512,512]{2,1,0:T(8,128)} %pad_maximum_fusion), channel_id=1, source_target_pairs={{0,2},{2,0},{1,3},{3,1},{4,6},{6,4},{5,7},{7,5},{8,10},{10,8},{9,1... | collective-permute-start | bytes 6291464 | tf_op jit(solution)/shard_map/ppermute | solution.py:15
  77.1 50.5 %collective-permute-start.2 = (f32[2,512,512]{2,1,0:T(8,128)}, f32[2,512,512]{2,1,0:T(8,128)}, u32[]{:S(2)}, u32[]{:S(2)}) collective-permute-start(f32[2,512,512]{2,1,0:T(8,128)} %pad_maximum_fusion.1), channel_id=1, source_target_pairs={{0,4},{4,0},{1,5},{5,1},{2,6},{6,2},{3,7},{7,3},{8,12},{12,8},{9,1... | collective-permute-start | bytes 6291464 | tf_op jit(solution)/shard_map/ppermute | solution.py:15
  138.9 49.6 %collective-permute-start.3 = (f32[2,512,512]{2,1,0:T(8,128)}, f32[2,512,512]{2,1,0:T(8,128)}, u32[]{:S(2)}, u32[]{:S(2)}) collective-permute-start(f32[2,512,512]{2,1,0:T(8,128)} %pad_maximum_fusion.2), channel_id=1, source_target_pairs={{0,8},{8,0},{1,9},{9,1},{2,10},{10,2},{3,11},{11,3},{4,12},{12,4},... | collective-permute-start | bytes 6291464 | tf_op jit(solution)/shard_map/ppermute | solution.py:15
  199.0 128.7 %all-gather.8.cloned.1.call-start = ((), (), s32[]{:S(2)}) async-start(), calls=%async_computation.2 | async-start | bytes 1114112 | tf_op jit(solution)/shard_map/all_gather | solution.py:76
  199.1 10.0 %collective-permute-start.4 = (bf16[2,32,512]{2,1,0:T(8,128)(2,1)}, bf16[2,32,512]{2,1,0:T(8,128)(2,1)S(1)}, u32[]{:S(2)}, u32[]{:S(2)}) collective-permute-start(bf16[2,32,512]{2,1,0:T(8,128)(2,1)} %fusion.50), channel_id=1, source_target_pairs={{0,496},{16,0},{32,16},{48,32},{64,48},{80,64},{96,80},{112,96},{1... | collective-permute-start | bytes 196616 | tf_op jit(solution)/shard_map/ppermute | solution.py:20
  268.5 123.9 %all-gather.10.cloned.1.call-start = ((), (), s32[]{:S(2)}) async-start(), calls=%async_computation.3 | async-start | bytes 1114112 | tf_op jit(solution)/shard_map/all_gather | solution.py:76
  268.6 8.2 %collective-permute-start.5 = (bf16[2,32,512]{2,1,0:T(8,128)(2,1)}, bf16[2,32,512]{2,1,0:T(8,128)(2,1)S(1)}, u32[]{:S(2)}, u32[]{:S(2)}) collective-permute-start(bf16[2,32,512]{2,1,0:T(8,128)(2,1)} %pad_maximum_fusion.3), channel_id=1, source_target_pairs={{0,480},{16,496},{32,0},{48,16},{64,32},{80,48},{96,64},{112,80},{... | collective-permute-start | bytes 196616 | tf_op jit(solution)/shard_map/ppermute | solution.py:20
  333.3 123.9 %all-gather.12.cloned.1.call-start = ((), (), s32[]{:S(2)}) async-start(), calls=%async_computation.4 | async-start | bytes 1114112 | tf_op jit(solution)/shard_map/all_gather | solution.py:76
  333.3 10.3 %collective-permute-start.6 = (bf16[2,32,512]{2,1,0:T(8,128)(2,1)}, bf16[2,32,512]{2,1,0:T(8,128)(2,1)S(1)}, u32[]{:S(2)}, u32[]{:S(2)}) collective-permute-start(bf16[2,32,512]{2,1,0:T(8,128)(2,1)} %pad_maximum_fusion.4), channel_id=1, source_target_pairs={{0,448},{16,464},{32,480},{48,496},{64,0},{80,16},{96,32},{112,48}... | collective-permute-start | bytes 196616 | tf_op jit(solution)/shard_map/ppermute | solution.py:20
  398.1 123.9 %all-gather.14.cloned.1.call-start = ((), (), s32[]{:S(2)}) async-start(), calls=%async_computation.5 | async-start | bytes 1114112 | tf_op jit(solution)/shard_map/all_gather | solution.py:76
  398.1 14.7 %collective-permute-start.7 = (bf16[2,32,512]{2,1,0:T(8,128)(2,1)}, bf16[2,32,512]{2,1,0:T(8,128)(2,1)S(1)}, u32[]{:S(2)}, u32[]{:S(2)}) collective-permute-start(bf16[2,32,512]{2,1,0:T(8,128)(2,1)} %pad_maximum_fusion.5), channel_id=1, source_target_pairs={{0,384},{16,400},{32,416},{48,432},{64,448},{80,464},{96,480},{112... | collective-permute-start | bytes 196616 | tf_op jit(solution)/shard_map/ppermute | solution.py:20
  462.9 15.8 %collective-permute-start.8 = (bf16[2,32,512]{2,1,0:T(8,128)(2,1)}, bf16[2,32,512]{2,1,0:T(8,128)(2,1)S(1)}, u32[]{:S(2)}, u32[]{:S(2)}) collective-permute-start(bf16[2,32,512]{2,1,0:T(8,128)(2,1)} %pad_maximum_fusion.6), channel_id=1, source_target_pairs={{0,256},{16,272},{32,288},{48,304},{64,320},{80,336},{96,352},{112... | collective-permute-start | bytes 196616 | tf_op jit(solution)/shard_map/ppermute | solution.py:20
Sparse Core Ops, SparseCore 0:
  199.1 63.7 all-gather.5
  268.6 58.9 all-gather.7
  333.4 58.9 all-gather.9
  398.2 58.9 all-gather.11
  463.0 58.9 all-gather.13
